TPU v7x, 32 devices: a whole 2x2x4 slice. The times are simulated.
32 devices in a mesh: group: 2 (over x), cell: 8 (over z, y), member: 2 (over core).
Axes of the slice: x: 2, y: 2, z: 4, core: 2. Of those that a mesh axis runs over, the one named last changes fastest.
Arguments:
- log_perm: float32 [16, 256, 16, 128], P('member', ('group', 'cell')), parts along dimension 1, may hold values from -4 to 4
- pressure: float32 [16, 256, 16, 128], P('member', ('group', 'cell')), parts along dimension 1, may hold values from -6 to 6
- saturation: float32 [16, 256, 16, 128], P('member', ('group', 'cell')), parts along dimension 1, may hold values from 0.1 to 0.9
- storage: float32 [256, 16, 128], P(('group', 'cell')), parts along dimension 0, may hold values from 0.05 to 0.5
- source: float32 [256, 16, 128], P(('group', 'cell')), parts along dimension 0, may hold values from -6 to 6
- active: int32 [256, 16, 128], P(('group', 'cell')), parts along dimension 0, may hold values 0 or 1
- wells: int32 [128], P('group'), parts along dimension 0, may hold values from 0 to 262143
- observed: float32 [256], P('group'), parts along dimension 0, may hold values from -6 to 6
- observation_variance: float32 [256], P('group'), parts along dimension 0, may hold values from 0.05 to 0.5
- noise: float32 [32, 128], P('group'), parts along dimension 0, may hold values from -5 to 5
Outputs:
- updated_perm: float32 [16, 256, 16, 128], P('member', ('group', 'cell')), parts along dimension 1
- pressure_out: float32 [16, 256, 16, 128], P('member', ('group', 'cell')), parts along dimension 1
- saturation_out: float32 [16, 256, 16, 128], P('member', ('group', 'cell')), parts along dimension 1
- predicted: float32 [32, 128], P(('group', 'member')), parts along dimension 0
There are 2 independent parts, one for each index of `group`. A program takes and returns all parts, laid end to end along the dimension named above; each array names one. Nothing has to cross between parts.
All inputs are finite; a program needn't handle non-finite values. No bound on the sum of `active` on one device may be relied on, other than what follows from the above.
Results may differ from a plain program's by a relative error of at most 0.0003.
Values sent between devices are 32-bit elements; how exact they have to be, the bound alone decides.
A program may use at most 128 MiB of HBM per device.

v0:
```python
import jax
import jax.numpy as jnp
from jax import lax
from jax.sharding import PartitionSpec as P

ITERS = 3


INFLATION_FACTOR = 4.0
TIME_STEP = 0.02


def with_halo(cells, sides, width):
    for axis, dim in sides:
        count = lax.axis_size(axis)
        ends = count - 1
        head = lax.slice_in_dim(cells, 0, width, axis=dim)
        tail = lax.slice_in_dim(cells, cells.shape[dim] - width, cells.shape[dim], axis=dim)
        cells = jnp.concatenate(
            [
                lax.ppermute(tail, axis, [(i, (i + 1) % count) for i in range(ends)]),
                cells,
                lax.ppermute(head, axis, [((i + 1) % count, i) for i in range(ends)]),
            ],
            axis=dim,
        )
    return cells


def pad_side(values):
    widths = [(0, 0)] * (values.ndim - 2) + [(1, 1), (1, 1)]
    return jnp.pad(values, widths)


def neighbours(padded_field):
    return [
        padded_field[..., 2:, 1:-1, 1:-1],
        padded_field[..., :-2, 1:-1, 1:-1],
        padded_field[..., 1:-1, 2:, 1:-1],
        padded_field[..., 1:-1, :-2, 1:-1],
        padded_field[..., 1:-1, 1:-1, 2:],
        padded_field[..., 1:-1, 1:-1, :-2],
    ]


def saturation_step(conduct, pres_field, near_pres, near_sat, saturation, storage):
    change = jnp.zeros_like(saturation)
    for link, pres_near, sat_near in zip(conduct, near_pres, near_sat):
        flux_value = link * (pres_near - pres_field)
        upwind_choice = jnp.where(flux_value > 0, sat_near, saturation)
        change = change + flux_value * upwind_choice * upwind_choice
    return saturation + TIME_STEP * change / storage[None]


def local(
    log_perm,
    pressure,
    saturation,
    storage,
    source,
    active,
    wells,
    observed,
    observation_variance,
    noise,
):
    mem_dev = log_perm.shape[0]
    members = mem_dev * lax.axis_size("member")
    first_own = lax.axis_index("member") * mem_dev
    scaled = active.astype(jnp.float32)[None] * jnp.exp(0.5 * log_perm)
    scaled_rim = pad_side(with_halo(scaled, (("cell", 1),), 1))
    conduct = [scaled * other for other in neighbours(scaled_rim)]
    balance = storage[None] + sum(conduct)
    rhs = storage[None] * pressure + source[None]
    pres_field = pressure
    for step in range(ITERS):
        pres_rim = pad_side(with_halo(pres_field, (("cell", 1),), 1))
        inflow = sum((link * other for link, other in zip(conduct, neighbours(pres_rim))))
        pres_field = (rhs + inflow) / balance
    stacked = pad_side(with_halo(jnp.stack([pres_field, saturation]), (("cell", 2),), 1))
    near_pres = neighbours(stacked[0])
    near_sat = neighbours(stacked[1])
    sat_new = saturation_step(conduct, pres_field, near_pres, near_sat, saturation, storage)
    cells_dev = active.shape[0] * active.shape[1] * active.shape[2]
    local_index = wells - lax.axis_index("cell") * cells_dev
    inside = ((local_index >= 0) & (local_index < cells_dev)).astype(jnp.float32)
    position = jnp.clip(local_index, 0, cells_dev - 1)
    flat_pres = pres_field.reshape(mem_dev, -1)
    flat_sat = sat_new.reshape(mem_dev, -1)
    found = jnp.concatenate(
        [
            jnp.take(flat_pres, position, axis=1) * inside[None],
            jnp.take(flat_sat, position, axis=1) * inside[None],
        ],
        axis=1,
    )
    own_data = lax.psum(found, "cell")
    predicted = lax.all_gather(own_data, "member", axis=0, tiled=True)
    centre = jnp.mean(predicted, axis=0)
    member_deviation = (predicted - centre[None]) / jnp.sqrt(jnp.float32(members - 1))
    covariance_matrix = jnp.dot(
        member_deviation.T, member_deviation, precision=lax.Precision.HIGHEST
    ) + INFLATION_FACTOR * jnp.diag(observation_variance)
    data_mismatch = (
        observed[None] + jnp.sqrt(INFLATION_FACTOR * observation_variance)[None] * noise - predicted
    )
    factor = jnp.linalg.cholesky(covariance_matrix)
    solved = jax.scipy.linalg.cho_solve((factor, True), data_mismatch.T)
    weights = jnp.dot(member_deviation, solved, precision=lax.Precision.HIGHEST)
    flat_perm = log_perm.reshape(mem_dev, -1)
    own_columns = lax.dynamic_slice_in_dim(weights, first_own, mem_dev, 1)
    tile_piece = lax.all_gather(log_perm, "member", axis=0, tiled=True)
    amount = tile_piece.shape[0]
    mixed = jnp.zeros_like(flat_perm) + jnp.dot(
        own_columns.T, tile_piece.reshape(amount, -1), precision=lax.Precision.HIGHEST
    )
    updated_perm = log_perm + (mixed / jnp.sqrt(jnp.float32(members - 1))).reshape(log_perm.shape)
    own_predicted = lax.dynamic_slice_in_dim(predicted, first_own, mem_dev, 0)
    return (updated_perm, pres_field, sat_new, own_predicted)


def solution(mesh):
    in_specs = (
        P("member", ("group", "cell"), None, None),
        P("member", ("group", "cell"), None, None),
        P("member", ("group", "cell"), None, None),
        P(("group", "cell"), None, None),
        P(("group", "cell"), None, None),
        P(("group", "cell"), None, None),
        P("group"),
        P("group"),
        P("group"),
        P("group", None),
    )
    out_specs = (
        P("member", ("group", "cell"), None, None),
        P("member", ("group", "cell"), None, None),
        P("member", ("group", "cell"), None, None),
        P(("group", "member"), None),
    )
    return jax.shard_map(local, mesh=mesh, in_specs=in_specs, out_specs=out_specs, check_vma=False)
```

profile of v0, /device:TPU:0, one launch (start us, length us, event | category | flops | bytes accessed | tf_op | source)
XLA Modules:
  0.0 174.9 jit_solution(6164691927104654758)
XLA Ops:
  10.9 5.5 %collective-permute-start.2 = (f32[8,1,16,128]{3,2,1,0:T(8,128)S(1)}, f32[8,1,16,128]{3,2,1,0:T(8,128)S(1)}, u32[]{:S(2)}, u32[]{:S(2)}) collective-permute-start(f32[8,1,16,128]{3,2,1,0:T(8,128)S(1)} %get-tuple-element.24), channel_id=1, source_target_pairs={{0,2},{2,4},{4,6},{6,8},{8,10},{10,12},{12,14},{1,3},{3,5},{5,7},{... | collective-permute-start | bytes 196616 | tf_op jit(solution)/shard_map/ppermute | solution.py:21
  18.6 5.6 %collective-permute-start.3 = (f32[8,1,16,128]{3,2,1,0:T(8,128)S(1)}, f32[8,1,16,128]{3,2,1,0:T(8,128)S(1)}, u32[]{:S(2)}, u32[]{:S(2)}) collective-permute-start(f32[8,1,16,128]{3,2,1,0:T(8,128)S(1)} %get-tuple-element.26), channel_id=1, source_target_pairs={{0,2},{2,4},{4,6},{6,8},{8,10},{10,12},{12,14},{1,3},{3,5},{5,7},{... | collective-permute-start | bytes 196616 | tf_op jit(solution)/shard_map/ppermute | solution.py:21
  24.3 1.6 select_maximum_fusion.9
  26.1 1.5 select_maximum_fusion.7
  27.7 3.3 %fusion.42 = (f32[8,16,16,128]{3,2,1,0:T(8,128)S(1)}, f32[8,16,16,128]{3,2,1,0:T(8,128)S(1)}, f32[8,16,16,128]{3,2,1,0:T(8,128)}, f32[8,16,16,128]{3,2,1,0:T(8,128)}, f32[8,16,16,128]{3,2,1,0:T(8,128)}) fusion(f32[8,18,18,130]{3,2,1,0:T(8,128)S(1)} %select_maximum_fusion.7, f32[8,16,16,128]{3,2,1,0:T(8,128)S(1)} %copy-done.1, ...), kind=kLoop, calls=%fused_computation.97 | loop fusion | flops 8126464 | bytes 16252928 | tf_op jit(solution)/shard_map/div | solution.py:79
  33.9 6.1 %collective-permute-start.5 = (f32[8,1,16,128]{3,2,1,0:T(8,128)}, f32[8,1,16,128]{3,2,1,0:T(8,128)}, u32[]{:S(2)}, u32[]{:S(2)}) collective-permute-start(f32[8,1,16,128]{3,2,1,0:T(8,128)} %get-tuple-element.22), channel_id=1, source_target_pairs={{0,2},{2,4},{4,6},{6,8},{8,10},{10,12},{12,14},{1,3},{3,5},{5,7},{... | collective-permute-start | bytes 196616 | tf_op jit(solution)/shard_map/ppermute | solution.py:21
  40.0 1.5 collective-permute-done.5
  41.5 2.6 %select_maximum_fusion.5 = f32[8,18,18,130]{3,2,1,0:T(8,128)S(1)} fusion(f32[8,1,16,128]{3,2,1,0:T(8,128)} %collective-permute-done.4, f32[8,16,16,128]{3,2,1,0:T(8,128)} %copy-done.10, f32[8,1,16,128]{3,2,1,0:T(8,128)} %collective-permute-done.5), kind=kLoop, calls=%fused_computation.21 | loop fusion | flops 5054400 | bytes 2527488 | tf_op jit(solution)/shard_map/concatenate | solution.py:19
  44.2 2.5 %fusion.33 = f32[8,16,16,128]{3,2,1,0:T(8,128)S(1)} fusion(f32[8,16,16,128]{3,2,1,0:T(8,128)S(1)} %copy-done.9, f32[8,18,18,130]{3,2,1,0:T(8,128)S(1)} %select_maximum_fusion.5, f32[8,16,16,128]{3,2,1,0:T(8,128)S(1)} %copy-done.7, f32[8,16,16,128]{3,2,1,0:T(8,128)S(1)} %copy-done.5, f32[8,16,16,128]{3,2,1,0:T(8,128)S(1)} %get-tuple-element.12, ...), kind=kLoop, calls=%fused_computation.82 | loop fusion | flops 7077888 | bytes 13107200 | tf_op jit(solution)/shard_map/div | solution.py:79
  48.2 5.8 %collective-permute-start.7 = (f32[8,1,16,128]{3,2,1,0:T(8,128)S(1)}, f32[8,1,16,128]{3,2,1,0:T(8,128)S(1)}, u32[]{:S(2)}, u32[]{:S(2)}) collective-permute-start(f32[8,1,16,128]{3,2,1,0:T(8,128)S(1)} %get-tuple-element.20), channel_id=1, source_target_pairs={{0,2},{2,4},{4,6},{6,8},{8,10},{10,12},{12,14},{1,3},{3,5},{5,7},{... | collective-permute-start | bytes 196616 | tf_op jit(solution)/shard_map/ppermute | solution.py:21
  55.9 1.5 select_maximum_fusion.3
  57.5 1.8 %fusion.24 = f32[8,16,16,128]{3,2,1,0:T(8,128)S(1)} fusion(f32[8,16,16,128]{3,2,1,0:T(8,128)S(1)} %copy-done.9, f32[8,18,18,130]{3,2,1,0:T(8,128)S(1)} %select_maximum_fusion.3, f32[8,16,16,128]{3,2,1,0:T(8,128)S(1)} %copy-done.7, f32[8,16,16,128]{3,2,1,0:T(8,128)S(1)} %copy-done.5, f32[8,16,16,128]{3,2,1,0:T(8,128)S(1)} %copy-done.3, ...), kind=kLoop, calls=%fused_computation.67 | loop fusion | flops 7077888 | bytes 13107200 | tf_op jit(solution)/shard_map/div | solution.py:79
  60.1 5.2 %collective-permute-start.8 = (f32[2,8,1,16,128]{4,3,2,1,0:T(8,128)}, f32[2,8,1,16,128]{4,3,2,1,0:T(8,128)S(1)}, u32[]{:S(2)}, u32[]{:S(2)}) collective-permute-start(f32[2,8,1,16,128]{4,3,2,1,0:T(8,128)} %get-tuple-element.18), channel_id=1, source_target_pairs={{0,2},{2,4},{4,6},{6,8},{8,10},{10,12},{12,14},{1,3},{3,5},{5,7},{... | collective-permute-start | bytes 393224 | tf_op jit(solution)/shard_map/ppermute | solution.py:21
  67.2 8.6 %copy.28 = f32[8,16,16,128]{0,3,2,1:T(8,128)} copy(f32[8,16,16,128]{3,2,1,0:T(8,128)S(1)} %fusion.24) | data formatting | bytes 2097152 | tf_op jit(solution)/shard_map/div | solution.py:79
  75.7 6.9 %gather_fusion = f32[64,8]{1,0:T(8,128)} fusion(f32[8,32768]{0,1:T(8,128)} %bitcast.36, s32[1024]{0:T(1024)S(1)} %pad_clamp_fusion), kind=kCustom, calls=%fused_computation.clone | custom fusion | bytes 4352 | tf_op jit(solution)/shard_map/jit(_take)/gather | solution.py:92
  83.5 4.3 %select_maximum_fusion = f32[2,8,18,18,130]{4,3,2,1,0:T(8,128)S(1)} fusion(f32[2,8,1,16,128]{4,3,2,1,0:T(8,128)} %collective-permute-done.9, f32[2,8,1,16,128]{4,3,2,1,0:T(8,128)S(1)} %collective-permute-done.8, f32[1,8,16,16,128]{4,3,2,1,0:T(8,128)S(1)} %bitcast.38, f32[1,8,16,16,128]{4,3,2,1,0:T(8,128)S(1)} %bitcast.34), kind=kLoop, calls=%fused_computation.7 | loop fusion | flops 12130560 | bytes 5054976 | tf_op jit(solution)/shard_map/concatenate | solution.py:19
  89.7 5.6 %fusion.15 = f32[8,16,16,128]{3,2,1,0:T(8,128)} fusion(f32[8,16,16,128]{3,2,1,0:T(8,128)} %param.14, f32[8,18,18,130]{3,2,1,0:T(8,128)S(1)} %get-tuple-element.17, f32[8,16,16,128]{3,2,1,0:T(8,128)} %get-tuple-element.15, f32[8,16,16,128]{3,2,1,0:T(8,128)S(1)} %fusion.24, f32[8,18,18,130]{3,2,1,0:T(8,128)S(1)} %get-tuple-element.16, ...), kind=kLoop, calls=%fused_computation.45 | loop fusion | flops 12582912 | bytes 21233664 | tf_op jit(solution)/shard_map/add | solution.py:52
  95.3 9.9 %copy.30 = f32[8,16,16,128]{0,3,2,1:T(8,128)} copy(f32[8,16,16,128]{3,2,1,0:T(8,128)} %fusion.15) | data formatting | bytes 2097152 | tf_op jit(solution)/shard_map/add | solution.py:52
  105.2 6.5 %gather_fusion.1 = f32[64,8]{1,0:T(8,128)S(1)} fusion(f32[8,32768]{0,1:T(8,128)} %bitcast.35, s32[1024]{0:T(1024)S(1)} %pad_clamp_fusion), kind=kCustom, calls=%fused_computation.1.clone | custom fusion | bytes 4352 | tf_op jit(solution)/shard_map/jit(_take)/gather | solution.py:93
  111.8 24.8 %psum.7 = f32[8,128]{1,0:T(8,128)S(1)} all-reduce(f32[8,128]{1,0:T(8,128)S(1)} %pad_maximum_fusion.10), channel_id=1, replica_groups=mesh['group'=2,'cell'=8,'member'=2] {'cell'}, use_global_device_ids=true, to_apply=%region_0.2 | all-reduce | flops 1024 | bytes 8192 | tf_op jit(solution)/shard_map/psum | solution.py:97
  136.5 2.0 %all_gather.6 = f32[16,128]{1,0:T(8,128)S(1)} all-gather(f32[8,128]{1,0:T(8,128)S(1)} %psum.7), channel_id=1, replica_groups=mesh['group'=2,'cell'=8,'member'=2] {'member'}, dimensions={0}, use_global_device_ids=true | all-gather | bytes 12288 | tf_op jit(solution)/shard_map/all_gather | solution.py:98
  139.0 11.7 %cholesky.16 = f32[128,128]{1,0:T(8,128)S(1)} custom-call(f32[128,128]{1,0:T(8,128)S(1)} %fusion.57), custom_call_target="Cholesky" | custom-call | tf_op jit(solution)/shard_map/jit(cholesky)/cholesky | solution.py:107
  152.1 9.8 %custom-call.10 = f32[1,128,128]{1,2,0:T(8,128)S(1)} custom-call(f32[1,128,128]{2,1,0:T(8,128)S(1)} %fusion.51), custom_call_target="InvertDiagBlocksLowerTriangular" | custom-call | tf_op jit(solution)/shard_map/jit(_cho_solve)/triangular_solve | solution.py:108
  163.0 3.8 %convolution_multiply_fusion = f32[8,32768]{1,0:T(8,128)S(1)} fusion(f32[2,8,256,128]{3,2,1,0:T(8,128)} %bitcast.40, f32[16,16]{0,1:T(8,128)S(1)} %fusion.61, s32[]{:T(128)S(6)} %select_n.51), kind=kOutput, calls=%fused_computation.2 | convolution fusion | flops 50593792 | bytes 3149828 | tf_op jit(solution)/shard_map/dot_general | solution.py:114
  (91 shorter events, 22.2 us)
Async XLA Ops:
  7.2 155.9 %all-gather.2.cloned.1.call-start = ((), (), s32[]{:S(2)}) async-start(), calls=%async_computation | async-start | bytes 3145728 | tf_op jit(solution)/shard_map/all_gather | solution.py:112
  8.1 18.0 %copy-start.1 = (f32[8,16,16,128]{3,2,1,0:T(8,128)S(1)}, f32[8,16,16,128]{3,2,1,0:T(8,128)}, u32[]{:S(2)}) copy-start(f32[8,16,16,128]{3,2,1,0:T(8,128)} %param.13) | copy-start | bytes 3145732
  9.6 14.6 %collective-permute-start = (f32[8,1,16,128]{3,2,1,0:T(8,128)S(1)}, f32[8,1,16,128]{3,2,1,0:T(8,128)S(1)}, u32[]{:S(2)}, u32[]{:S(2)}) collective-permute-start(f32[8,1,16,128]{3,2,1,0:T(8,128)S(1)} %get-tuple-element.25), channel_id=1, source_target_pairs={{2,0},{4,2},{6,4},{8,6},{10,8},{12,10},{14,12},{3,1},{5,3},{7,5},{... | collective-permute-start | bytes 196616 | tf_op jit(solution)/shard_map/ppermute | solution.py:23
  10.9 13.3 %collective-permute-start.2 = (f32[8,1,16,128]{3,2,1,0:T(8,128)S(1)}, f32[8,1,16,128]{3,2,1,0:T(8,128)S(1)}, u32[]{:S(2)}, u32[]{:S(2)}) collective-permute-start(f32[8,1,16,128]{3,2,1,0:T(8,128)S(1)} %get-tuple-element.24), channel_id=1, source_target_pairs={{0,2},{2,4},{4,6},{6,8},{8,10},{10,12},{12,14},{1,3},{3,5},{5,7},{... | collective-permute-start | bytes 196616 | tf_op jit(solution)/shard_map/ppermute | solution.py:21
  17.3 8.5 %collective-permute-start.1 = (f32[8,1,16,128]{3,2,1,0:T(8,128)S(1)}, f32[8,1,16,128]{3,2,1,0:T(8,128)S(1)}, u32[]{:S(2)}, u32[]{:S(2)}) collective-permute-start(f32[8,1,16,128]{3,2,1,0:T(8,128)S(1)} %get-tuple-element.27), channel_id=1, source_target_pairs={{2,0},{4,2},{6,4},{8,6},{10,8},{12,10},{14,12},{3,1},{5,3},{7,5},{... | collective-permute-start | bytes 196616 | tf_op jit(solution)/shard_map/ppermute | solution.py:23
  18.6 9.0 %copy-start.15 = (f32[16,16,128]{2,1,0:T(8,128)S(1)}, f32[16,16,128]{2,1,0:T(8,128)}, u32[]{:S(2)}) copy-start(f32[16,16,128]{2,1,0:T(8,128)} %param.15) | copy-start | bytes 393220
  18.6 7.5 %collective-permute-start.3 = (f32[8,1,16,128]{3,2,1,0:T(8,128)S(1)}, f32[8,1,16,128]{3,2,1,0:T(8,128)S(1)}, u32[]{:S(2)}, u32[]{:S(2)}) collective-permute-start(f32[8,1,16,128]{3,2,1,0:T(8,128)S(1)} %get-tuple-element.26), channel_id=1, source_target_pairs={{0,2},{2,4},{4,6},{6,8},{8,10},{10,12},{12,14},{1,3},{3,5},{5,7},{... | collective-permute-start | bytes 196616 | tf_op jit(solution)/shard_map/ppermute | solution.py:21
  30.9 15.8 %copy-start.2 = (f32[8,16,16,128]{3,2,1,0:T(8,128)}, f32[8,16,16,128]{3,2,1,0:T(8,128)S(1)}, u32[]{:S(2)}) copy-start(f32[8,16,16,128]{3,2,1,0:T(8,128)S(1)} %get-tuple-element.12) | copy-start | bytes 3145732
  32.6 7.4 %collective-permute-start.4 = (f32[8,1,16,128]{3,2,1,0:T(8,128)}, f32[8,1,16,128]{3,2,1,0:T(8,128)}, u32[]{:S(2)}, u32[]{:S(2)}) collective-permute-start(f32[8,1,16,128]{3,2,1,0:T(8,128)} %get-tuple-element.23), channel_id=1, source_target_pairs={{2,0},{4,2},{6,4},{8,6},{10,8},{12,10},{14,12},{3,1},{5,3},{7,5},{... | collective-permute-start | bytes 196616 | tf_op jit(solution)/shard_map/ppermute | solution.py:23
  33.9 7.7 %collective-permute-start.5 = (f32[8,1,16,128]{3,2,1,0:T(8,128)}, f32[8,1,16,128]{3,2,1,0:T(8,128)}, u32[]{:S(2)}, u32[]{:S(2)}) collective-permute-start(f32[8,1,16,128]{3,2,1,0:T(8,128)} %get-tuple-element.22), channel_id=1, source_target_pairs={{0,2},{2,4},{4,6},{6,8},{8,10},{10,12},{12,14},{1,3},{3,5},{5,7},{... | collective-permute-start | bytes 196616 | tf_op jit(solution)/shard_map/ppermute | solution.py:21
  44.2 9.8 %copy-start.22 = (s32[64]{0:T(128)S(1)}, s32[64]{0:T(128)}, u32[]{:S(2)}) copy-start(s32[64]{0:T(128)} %param.18) | copy-start | bytes 772
  46.8 10.7 %copy-start.3 = (f32[8,16,16,128]{3,2,1,0:T(8,128)S(1)}, f32[8,16,16,128]{3,2,1,0:T(8,128)}, u32[]{:S(2)}) copy-start(f32[8,16,16,128]{3,2,1,0:T(8,128)} %copy-done.2) | copy-start | bytes 3145732
  46.8 7.8 %collective-permute-start.6 = (f32[8,1,16,128]{3,2,1,0:T(8,128)S(1)}, f32[8,1,16,128]{3,2,1,0:T(8,128)S(1)}, u32[]{:S(2)}, u32[]{:S(2)}) collective-permute-start(f32[8,1,16,128]{3,2,1,0:T(8,128)S(1)} %get-tuple-element.21), channel_id=1, source_target_pairs={{2,0},{4,2},{6,4},{8,6},{10,8},{12,10},{14,12},{3,1},{5,3},{7,5},{... | collective-permute-start | bytes 196616 | tf_op jit(solution)/shard_map/ppermute | solution.py:23
  48.2 7.7 %collective-permute-start.7 = (f32[8,1,16,128]{3,2,1,0:T(8,128)S(1)}, f32[8,1,16,128]{3,2,1,0:T(8,128)S(1)}, u32[]{:S(2)}, u32[]{:S(2)}) collective-permute-start(f32[8,1,16,128]{3,2,1,0:T(8,128)S(1)} %get-tuple-element.20), channel_id=1, source_target_pairs={{0,2},{2,4},{4,6},{6,8},{8,10},{10,12},{12,14},{1,3},{3,5},{5,7},{... | collective-permute-start | bytes 196616 | tf_op jit(solution)/shard_map/ppermute | solution.py:21
  57.5 9.1 %copy-start.18 = (f32[128]{0:T(128)S(1)}, f32[128]{0:T(128)}, u32[]{:S(2)}) copy-start(f32[128]{0:T(128)} %param.20) | copy-start | bytes 1540
  59.3 29.1 %copy-start = (f32[8,16,16,128]{3,2,1,0:T(8,128)}, f32[8,16,16,128]{3,2,1,0:T(8,128)S(1)}, u32[]{:S(2)}) copy-start(f32[8,16,16,128]{3,2,1,0:T(8,128)S(1)} %fusion.24) | copy-start | bytes 3145732
  60.1 23.4 %collective-permute-start.8 = (f32[2,8,1,16,128]{4,3,2,1,0:T(8,128)}, f32[2,8,1,16,128]{4,3,2,1,0:T(8,128)S(1)}, u32[]{:S(2)}, u32[]{:S(2)}) collective-permute-start(f32[2,8,1,16,128]{4,3,2,1,0:T(8,128)} %get-tuple-element.18), channel_id=1, source_target_pairs={{0,2},{2,4},{4,6},{6,8},{8,10},{10,12},{12,14},{1,3},{3,5},{5,7},{... | collective-permute-start | bytes 393224 | tf_op jit(solution)/shard_map/ppermute | solution.py:21
  65.2 18.2 %collective-permute-start.9 = (f32[2,8,1,16,128]{4,3,2,1,0:T(8,128)}, f32[2,8,1,16,128]{4,3,2,1,0:T(8,128)}, u32[]{:S(2)}, u32[]{:S(2)}) collective-permute-start(f32[2,8,1,16,128]{4,3,2,1,0:T(8,128)} %get-tuple-element.19), channel_id=1, source_target_pairs={{2,0},{4,2},{6,4},{8,6},{10,8},{12,10},{14,12},{3,1},{5,3},{7,5},{... | collective-permute-start | bytes 393224 | tf_op jit(solution)/shard_map/ppermute | solution.py:23
  67.1 16.3 %copy-start.14 = (f32[8,16,16,128]{3,2,1,0:T(8,128)S(1)}, f32[8,16,16,128]{3,2,1,0:T(8,128)}, u32[]{:S(2)}) copy-start(f32[8,16,16,128]{3,2,1,0:T(8,128)} %param.14) | copy-start | bytes 3145732
  95.3 16.4 %copy-start.19 = (f32[64]{0:T(128)S(1)}, f32[64]{0:T(128)}, u32[]{:S(2)}) copy-start(f32[64]{0:T(128)} %get-tuple-element.30) | copy-start | bytes 772
  95.3 67.2 %copy-start.17 = (f32[16,128]{1,0:T(8,128)S(1)}, f32[16,128]{1,0:T(8,128)}, u32[]{:S(2)}) copy-start(f32[16,128]{1,0:T(8,128)} %param.21) | copy-start | bytes 24580
  95.3 67.2 %copy-start.20 = (f32[128]{0:T(128)S(1)}, f32[128]{0:T(128)}, u32[]{:S(2)}) copy-start(f32[128]{0:T(128)} %param.19) | copy-start | bytes 1540
  95.3 67.2 %copy-start.21 = (f32[128]{0:T(128)S(1)}, f32[128]{0:T(128)}, u32[]{:S(2)}) copy-start(f32[128]{0:T(128)} %multiply_sqrt_fusion) | copy-start | bytes 1540
  105.2 61.7 %copy-start.12 = (f32[8,16,16,128]{3,2,1,0:T(8,128)S(1)}, f32[8,16,16,128]{3,2,1,0:T(8,128)}, u32[]{:S(2)}) copy-start(f32[8,16,16,128]{3,2,1,0:T(8,128)} %param.12) | copy-start | bytes 3145732
  (10 other events, 33.2 us)
Sparse Core Ops, SparseCore 0:
  40.1 13.0 all-gather.1
where the time goes:
time: 176 us; the launch traced here: 175 us
  other arithmetic  53.3 us (30%)
  local copies, waits for them, and re-layouts  37.9 us (22%)
  starting transfers between devices  34.7 us (20%)
  blocking collectives  26.7 us (15%)
  between operations  14.5 us (8%)
  matrix products  4.6 us (3%)
  waiting for transfers between devices  3.19 us (2%)
    ppermute x5, starting transfers between devices, with_halo(): lax.ppermute(tail, axis, [(i, (i + 1) % count) for i in range(ends)])  28.1 us
    psum x1, blocking collectives, local(): own_data = lax.psum(found, 'cell')  24.8 us
    another operation x3, other arithmetic, local(): factor = jnp.linalg.cholesky(covariance_matrix)  12.4 us
    concatenate x5, other arithmetic, with_halo(): jnp.concatenate([lax.ppermute(tail, axis, [(i, (i + 1) % count) for i in...  11.6 us
    another operation x2, other arithmetic, local(): solved = jax.scipy.linalg.cho_solve((factor, True), data_mismatch.T)  10.5 us
    add x1, local copies, waits for them, and re-layouts, saturation_step(): return saturation + TIME_STEP * change / storage[None]  9.86 us
    div x1, local copies, waits for them, and re-layouts, local(): pres_field = (rhs + inflow) / balance  8.56 us
    gather x2, local copies, waits for them, and re-layouts, local(): jnp.take(flat_pres, position, axis=1) * inside[None]  7.76 us
  transfers between devices with their start and end apart: 11, of which 3 were waited for; matrix products, arithmetic and copies ran while one was open for 46% of the time, Pallas kernels for 0%

commit v1 on v0

v1 whole, which is shorter than its diff:
```python
import functools
import jax
import jax.numpy as jnp
from jax import lax
from jax.experimental import pallas as pl
from jax.experimental.pallas import tpu as pltpu
from jax.sharding import PartitionSpec as P

ITERS = 3
INFLATION_FACTOR = 4.0
TIME_STEP = 0.02
MESH = pl.DeviceIdType.MESH
LP, PR, SAT, Q1, Q2, P3 = range(6)


def kernel(
    ncell,
    lp_hbm, pr_hbm, sat_hbm, sto_hbm, src_hbm, act_hbm, wells, obs, var, noise,
    upd_out, pr_out, sat_out, pred_out,
    lp, lp_peer, pr, sat, sto, src, act,
    s, qa, qb, rhs, rbal, p3, snew, upd,
    halo, act_halo, s_halo, q0_halo, found, wcol,
    load_sems, out_sems, send_sems, recv_sems, act_send, act_recv,
    peer_send, peer_recv, found_send, found_recv,
):
    md, nx, cy, cz = lp.shape
    cell = lax.axis_index("cell")
    mem = lax.axis_index("member")
    other = 1 - mem
    has_left = cell > 0
    has_right = cell < ncell - 1
    left = jnp.maximum(cell - 1, 0)
    right = jnp.minimum(cell + 1, ncell - 1)

    loads = [
        pltpu.make_async_copy(a, b, load_sems.at[i])
        for i, (a, b) in enumerate(
            [(act_hbm, act), (lp_hbm, lp), (pr_hbm, pr), (sto_hbm, sto), (src_hbm, src), (sat_hbm, sat)]
        )
    ]
    for c in loads:
        c.start()

    barrier = pltpu.get_barrier_semaphore()

    def greet(k, carry):
        to = lax.rem(cell + k, ncell)
        pl.semaphore_signal(barrier, inc=1, device_id={"cell": to, "member": other}, device_id_type=MESH)

        @pl.when(k > 0)
        def _():
            pl.semaphore_signal(barrier, inc=1, device_id={"cell": to, "member": mem}, device_id_type=MESH)

        return carry

    lax.fori_loop(0, ncell, greet, 0)
    pl.semaphore_wait(barrier, 2 * ncell - 1)

    def remote(source, dest, ssem, rsem, to):
        return pltpu.make_async_remote_copy(
            src_ref=source, dst_ref=dest, send_sem=ssem, recv_sem=rsem,
            device_id={"cell": to}, device_id_type=MESH,
        )

    def edge_copy(f, side, ref):
        x = nx - 1 if side == 0 else 0
        to = right if side == 0 else left
        return remote(ref.at[:, x], halo.at[f, side], send_sems.at[f, side], recv_sems.at[f, side], to)

    def act_copy(side):
        x = nx - 1 if side == 0 else 0
        to = right if side == 0 else left
        return remote(act_hbm.at[x], act_halo.at[side], act_send.at[side], act_recv.at[side], to)

    def send_edges(f, ref):
        @pl.when(has_left)
        def _():
            edge_copy(f, 1, ref).start()

        @pl.when(has_right)
        def _():
            edge_copy(f, 0, ref).start()

    def wait_edges(f, ref):
        @pl.when(has_left)
        def _():
            edge_copy(f, 0, ref).wait_recv()

        @pl.when(has_right)
        def _():
            edge_copy(f, 1, ref).wait_recv()

    def sent_edges(f, ref):
        @pl.when(has_left)
        def _():
            edge_copy(f, 1, ref).wait_send()

        @pl.when(has_right)
        def _():
            edge_copy(f, 0, ref).wait_send()

    @pl.when(has_left)
    def _():
        act_copy(1).start()

    @pl.when(has_right)
    def _():
        act_copy(0).start()

    send_edges(LP, lp_hbm)
    send_edges(PR, pr_hbm)
    send_edges(SAT, sat_hbm)
    peer = pltpu.make_async_remote_copy(
        src_ref=lp_hbm, dst_ref=lp_peer, send_sem=peer_send, recv_sem=peer_recv,
        device_id={"member": other}, device_id_type=MESH,
    )
    peer.start()

    @pl.when(jnp.logical_not(has_left))
    def _():
        for f in range(6):
            halo[f, 0] = jnp.zeros((md, cy, cz), jnp.float32)
        s_halo[0] = jnp.zeros((md, cy, cz), jnp.float32)

    @pl.when(jnp.logical_not(has_right))
    def _():
        for f in range(6):
            halo[f, 1] = jnp.zeros((md, cy, cz), jnp.float32)
        s_halo[1] = jnp.zeros((md, cy, cz), jnp.float32)

    lane = lax.broadcasted_iota(jnp.int32, (1, cy, cz), 2)
    row = lax.broadcasted_iota(jnp.int32, (1, cy, cz), 1)

    def z_up(v):
        return pltpu.roll(v, cz - 1, 2)

    def z_down(v):
        return pltpu.roll(v, 1, 2)

    def y_up(v):
        return pltpu.roll(v, cy - 1, 1)

    def y_down(v):
        return pltpu.roll(v, 1, 1)

    def plane_sum(q):
        return (
            jnp.where(lane == cz - 1, 0.0, z_up(q))
            + jnp.where(lane == 0, 0.0, z_down(q))
            + jnp.where(row == cy - 1, 0.0, y_up(q))
            + jnp.where(row == 0, 0.0, y_down(q))
        )

    loads[0].wait()
    loads[1].wait()
    for i in (2, 3, 4):
        loads[i].wait()

    def prepare(x, carry):
        sc = act[x].astype(jnp.float32)[None] * jnp.exp(0.5 * lp[:, x])
        s[:, x] = sc
        pc = pr[:, x]
        qa[:, x] = sc * pc
        rhs[:, x] = sto[x][None] * pc + src[x][None]
        return carry

    lax.fori_loop(0, nx, prepare, 0)

    def balance_at(x, below, above):
        sc = s[:, x]
        total = sto[x][None] + sc * (below + above + plane_sum(sc))
        rbal[:, x] = 1.0 / total

    def sweep_at(x, below, above, old, new, last):
        sc = s[:, x]
        p = (rhs[:, x] + sc * (below + above + plane_sum(old[:, x]))) * rbal[:, x]
        new[:, x] = p if last else sc * p

    def interior(f):
        def step(x, carry):
            f(x)
            return carry

        lax.fori_loop(1, nx - 1, step, 0)

    def first_inside(x):
        balance_at(x, s[:, x - 1], s[:, x + 1])
        sweep_at(x, qa[:, x - 1], qa[:, x + 1], qa, qb, False)

    interior(first_inside)

    for side, there in ((0, has_left), (1, has_right)):
        @pl.when(there)
        def _(side=side):
            act_copy(side).wait_recv()
            edge_copy(LP, side, lp_hbm).wait_recv()
            edge_copy(PR, side, pr_hbm).wait_recv()
            s_halo[side] = act_halo[side].astype(jnp.float32)[None] * jnp.exp(0.5 * halo[LP, side])

        q0_halo[side] = s_halo[side] * halo[PR, side]

    end = nx - 1
    balance_at(0, s_halo[0], s[:, 1])
    sweep_at(0, q0_halo[0], qa[:, 1], qa, qb, False)
    balance_at(end, s[:, end - 1], s_halo[1])
    sweep_at(end, qa[:, end - 1], q0_halo[1], qa, qb, False)
    send_edges(Q1, qb)

    interior(lambda x: sweep_at(x, qb[:, x - 1], qb[:, x + 1], qb, qa, False))
    wait_edges(Q1, qb)
    sweep_at(0, halo[Q1, 0], qb[:, 1], qb, qa, False)
    sweep_at(end, qb[:, end - 1], halo[Q1, 1], qb, qa, False)
    send_edges(Q2, qa)

    interior(lambda x: sweep_at(x, qa[:, x - 1], qa[:, x + 1], qa, p3, True))
    wait_edges(Q2, qa)
    sweep_at(0, halo[Q2, 0], qa[:, 1], qa, p3, True)
    sweep_at(end, qa[:, end - 1], halo[Q2, 1], qa, p3, True)
    send_edges(P3, p3)
    put_p = pltpu.make_async_copy(p3, pr_out, out_sems.at[0])
    put_p.start()
    loads[5].wait()

    def face(sn, pn, tn, pc, tc):
        d = pn - pc
        return sn * (d * jnp.where(d > 0, tn, tc))

    def saturate_at(x, below, above):
        sc = s[:, x]
        pc = p3[:, x]
        raw = sat[:, x]
        tc = raw * raw
        bs, bp, bt = below
        as_, ap, at = above
        change = face(bs, bp, bt * bt, pc, tc) + face(as_, ap, at * at, pc, tc)
        gz = sc * face(jnp.where(lane == cz - 1, 0.0, z_up(sc)), z_up(pc), z_up(tc), pc, tc)
        gy = sc * face(jnp.where(row == cy - 1, 0.0, y_up(sc)), y_up(pc), y_up(tc), pc, tc)
        change = sc * change + (gz - z_down(gz)) + (gy - y_down(gy))
        snew[:, x] = raw + change * (TIME_STEP / sto[x])[None]

    def at_x(x):
        return s[:, x], p3[:, x], sat[:, x]

    interior(lambda x: saturate_at(x, at_x(x - 1), at_x(x + 1)))

    nw = wells.shape[0]
    cells_dev = nx * cy * cz
    col = lax.broadcasted_iota(jnp.int32, (md, 2 * nw), 1)
    p3_rows = p3.reshape(md * nx * cy, cz)
    sn_rows = snew.reshape(md * nx * cy, cz)

    def gather(rows, first):
        def one(w, acc):
            at = wells[w] - cell * cells_dev
            inside = jnp.logical_and(at >= 0, at < cells_dev)
            at = jnp.clip(at, 0, cells_dev - 1)
            line = at // cz
            z = at - line * cz
            v = rows[pl.ds(line, md, stride=nx * cy), :]
            v = pltpu.roll(v, lax.rem(first + w - z + cz, cz), 1)
            keep = jnp.where(inside, w + first, -1)
            return jnp.where(col == keep, v, acc)

        return one

    acc = lax.fori_loop(0, nw, gather(p3_rows, 0), jnp.zeros((md, 2 * nw), jnp.float32), unroll=8)

    wait_edges(SAT, sat_hbm)
    wait_edges(P3, p3)
    saturate_at(0, (s_halo[0], halo[P3, 0], halo[SAT, 0]), at_x(1))
    saturate_at(end, at_x(end - 1), (s_halo[1], halo[P3, 1], halo[SAT, 1]))
    put_s = pltpu.make_async_copy(snew, sat_out, out_sems.at[1])
    put_s.start()
    acc = lax.fori_loop(0, nw, gather(sn_rows, nw), acc, unroll=8)
    found[0, 0] = acc

    def found_copy(k, m):
        return pltpu.make_async_remote_copy(
            src_ref=found.at[0, 0], dst_ref=found.at[m, k],
            send_sem=found_send.at[m, k], recv_sem=found_recv.at[m, k],
            device_id={"cell": lax.rem(cell + k, ncell), "member": mem if m == 0 else other},
            device_id_type=MESH,
        )

    def each_found(act_on):
        def step(k, carry):
            act_on(found_copy(k, 1))

            @pl.when(k > 0)
            def _():
                act_on(found_copy(k, 0))

            return carry

        lax.fori_loop(0, ncell, step, 0)

    each_found(lambda c: c.start())
    each_found(lambda c: c.wait_recv())

    own = found[0, 0]
    far = found[1, 0]
    for k in range(1, ncell):
        own = own + found[0, k]
        far = far + found[1, k]
    pred_out[...] = own

    members = 2 * md
    nd = 2 * nw
    root = float(members - 1) ** 0.5
    both = jnp.concatenate([own, far], axis=0)
    spread = (both - jnp.mean(both, axis=0, keepdims=True)) * (1.0 / root)
    dvar = INFLATION_FACTOR * var[...]
    first = pl.multiple_of(mem * md, md)
    misfit = obs[...] + jnp.sqrt(dvar) * noise[pl.ds(first, md), :] - own
    stack = jnp.concatenate([spread, misfit, jnp.zeros((nd - 3 * md, nd), jnp.float32)], axis=0)
    aug = lax.dot_general(
        spread / dvar, stack, (((1,), (1,)), ((), ())),
        precision=lax.Precision.HIGHEST, preferred_element_type=jnp.float32,
    )
    rid = lax.broadcasted_iota(jnp.int32, (members, nd), 0)
    cid = lax.broadcasted_iota(jnp.int32, (members, nd), 1)
    aug = aug + jnp.where(rid == cid, 1.0, 0.0)
    for k in range(members):
        line = aug[k : k + 1, :] / aug[k : k + 1, k : k + 1]
        aug = jnp.where(rid == k, line, aug - aug[:, k : k + 1] * line)
    for j in range(md):
        wcol[j] = jnp.broadcast_to(aug[:, members + j : members + j + 1] * (1.0 / root), (members, cz))

    peer.wait_recv()
    parts = 4
    share = nx // parts

    def put_u(i):
        return pltpu.make_async_copy(
            upd.at[:, pl.ds(i * share, share)], upd_out.at[:, pl.ds(i * share, share)], out_sems.at[2 + i]
        )

    def mix(x, carry):
        fields = [lp[i, x] for i in range(md)] + [lp_peer[i, x] for i in range(md)]
        for j in range(md):
            total = fields[j]
            for i in range(members):
                total = total + wcol[j, i : i + 1, :] * fields[i]
            upd[j, x] = total
        return carry

    for i in range(parts):
        lax.fori_loop(i * share, (i + 1) * share, mix, 0)
        put_u(i).start()

    each_found(lambda c: c.wait_send())
    peer.wait_send()
    for f, ref in ((LP, lp_hbm), (PR, pr_hbm), (SAT, sat_hbm), (Q1, qb), (Q2, qa), (P3, p3)):
        sent_edges(f, ref)

    @pl.when(has_left)
    def _():
        act_copy(1).wait_send()

    @pl.when(has_right)
    def _():
        act_copy(0).wait_send()

    put_p.wait()
    put_s.wait()
    for i in range(parts):
        put_u(i).wait()


def local(
    log_perm, pressure, saturation, storage, source, active, wells, observed, observation_variance, noise,
):
    md, nx, cy, cz = log_perm.shape
    ncell = lax.axis_size("cell")
    nd = observed.shape[0]
    field = (md, nx, cy, cz)
    plane = (nx, cy, cz)
    f32 = jnp.float32
    any_spec = pl.BlockSpec(memory_space=pl.ANY)
    vmem_spec = pl.BlockSpec(memory_space=pltpu.VMEM)
    dma = pltpu.SemaphoreType.DMA
    return pl.pallas_call(
        functools.partial(kernel, ncell),
        out_shape=[jax.ShapeDtypeStruct(field, f32)] * 3 + [jax.ShapeDtypeStruct((md, nd), f32)],
        in_specs=[any_spec] * 6 + [pl.BlockSpec(memory_space=pltpu.SMEM)] + [vmem_spec] * 3,
        out_specs=[any_spec] * 3 + [vmem_spec],
        scratch_shapes=[
            pltpu.VMEM(field, f32), pltpu.VMEM(field, f32), pltpu.VMEM(field, f32), pltpu.VMEM(field, f32),
            pltpu.VMEM(plane, f32), pltpu.VMEM(plane, f32), pltpu.VMEM(plane, jnp.int32),
            *[pltpu.VMEM(field, f32) for _ in range(8)],
            pltpu.VMEM((6, 2, md, cy, cz), f32),
            pltpu.VMEM((2, cy, cz), jnp.int32),
            pltpu.VMEM((2, md, cy, cz), f32),
            pltpu.VMEM((2, md, cy, cz), f32),
            pltpu.VMEM((2, ncell, md, nd), f32),
            pltpu.VMEM((md, 2 * md, cz), f32),
            dma((6,)), dma((6,)), dma((6, 2)), dma((6, 2)), dma((2,)), dma((2,)),
            dma, dma, dma((2, ncell)), dma((2, ncell)),
        ],
        compiler_params=pltpu.CompilerParams(
            collective_id=0, has_side_effects=True, vmem_limit_bytes=58 * 1024 * 1024
        ),
    )(
        log_perm, pressure, saturation, storage, source, active, wells,
        observed.reshape(1, nd), observation_variance.reshape(1, nd), noise,
    )


def solution(mesh):
    block = P("member", ("group", "cell"), None, None)
    shared = P(("group", "cell"), None, None)
    in_specs = (block, block, block, shared, shared, shared, P("group"), P("group"), P("group"), P("group", None))
    out_specs = (block, block, block, P(("group", "member"), None))
    return jax.shard_map(local, mesh=mesh, in_specs=in_specs, out_specs=out_specs, check_vma=False)
```

time: 176 us -> 45.9 us (0.26)
  other arithmetic: 53.3 us -> 0 us
  Pallas kernels: 0 us -> 39.5 us
  starting transfers between devices: 34.7 us -> 0 us
  local copies, waits for them, and re-layouts: 37.9 us -> 5.53 us
  blocking collectives: 26.7 us -> 0 us
  between operations: 14.5 us -> 0.65 us
  matrix products: 4.6 us -> 0 us
  waiting for transfers between devices: 3.19 us -> 0 us
    pallas_call x0 -> x1, Pallas kernels: none -> 39.5 us  [local(): pl.pallas_call(functools.partial(kernel, ncell), out_shape=[jax.ShapeDtyp...]
    ppermute x10 -> x0, starting transfers between devices: 34.7 us -> none  [the longest x5 28.1 us: with_halo(): lax.ppermute(tail, axis, [(i, (i + 1) % count) for i in range(ends)])]
    psum x1 -> x0, blocking collectives: 24.8 us -> none  [local(): own_data = lax.psum(found, 'cell')]
    another operation x5 -> x0, other arithmetic: 22.9 us -> none  [the longest x3 12.4 us: local(): factor = jnp.linalg.cholesky(covariance_matrix)]
    gather x4 -> x0, local copies, waits for them, and re-layouts: 14.3 us -> none  [the longest x2 7.76 us: local(): jnp.take(flat_pres, position, axis=1) * inside[None]]
    concatenate x6 -> x0, other arithmetic: 11.6 us -> none  [the longest x5 11.6 us: with_halo(): jnp.concatenate([lax.ppermute(tail, axis, [(i, (i + 1) % count) for i in...]
    add x1 -> x0, local copies, waits for them, and re-layouts: 9.86 us -> none  [saturation_step(): return saturation + TIME_STEP * change / storage[None]]
    div x1 -> x0, local copies, waits for them, and re-layouts: 8.56 us -> none  [local(): pres_field = (rhs + inflow) / balance]
  transfers between devices with their start and end apart: 11 -> 0, of which waited for: 3 -> 0; matrix products, arithmetic and copies ran while one was open for 46% -> 0% of each run, Pallas kernels for 0% -> 0%
where the time goes in v1:
time: 45.9 us; the launch traced here: 45.7 us
  Pallas kernels  39.5 us (86%)
  local copies, waits for them, and re-layouts  5.53 us (12%)
  between operations  0.65 us (1%)
    pallas_call x1, Pallas kernels, local(): pl.pallas_call(functools.partial(kernel, ncell), out_shape=[jax.ShapeDtyp...  39.5 us
    unnamed x10, local copies, waits for them, and re-layouts  5.53 us

profile of v1, /device:TPU:0, one launch (start us, length us, event | category | flops | bytes accessed | tf_op | source)
XLA Modules:
  0.0 45.7 jit_solution(12093716186675659765)
XLA Ops:
  0.6 39.5 %shard_map.129 = (f32[8,16,16,128]{3,2,1,0:T(8,128)}, f32[8,16,16,128]{3,2,1,0:T(8,128)}, f32[8,16,16,128]{3,2,1,0:T(8,128)}, f32[8,128]{1,0:T(8,128)}) custom-call(f32[8,16,16,128]{3,2,1,0:T(8,128)} %lp_hbm.1, f32[8,16,16,128]{3,2,1,0:T(8,128)} %pr_hbm.1, f32[8,16,16,128]{3,2,1,0:T(8,128)} %sat_hbm.1, f32[16,16,128]{2,1,0:T(8,128)} %sto_hbm.1, ...), custom_call_target="tpu_custom_call" | custom-call | tf_op jit(solution)/shard_map/pallas_call | solution.py:382
  40.2 0.0 copy-start.1
  40.2 2.4 %copy.18 = f32[8,16,16,128]{3,2,1,0:T(8,128)} copy(f32[8,16,16,128]{3,2,1,0:T(8,128)} %get-tuple-element.8) | data formatting | bytes 2097152
  42.5 0.0 copy-done.1
  42.5 0.0 copy-start
  42.5 1.0 %copy.19 = f32[8,16,16,128]{3,2,1,0:T(8,128)} copy(f32[8,16,16,128]{3,2,1,0:T(8,128)S(1)} %copy-done.1) | data formatting | bytes 2097152
  43.5 0.6 %copy-done = f32[8,16,16,128]{3,2,1,0:T(8,128)S(1)} copy-done((f32[8,16,16,128]{3,2,1,0:T(8,128)S(1)}, f32[8,16,16,128]{3,2,1,0:T(8,128)}, u32[]{:S(2)}) %copy-start) | copy-done | bytes 1048600
  44.1 0.0 copy-start.2
  44.1 1.0 %copy.20 = f32[8,16,16,128]{3,2,1,0:T(8,128)} copy(f32[8,16,16,128]{3,2,1,0:T(8,128)S(1)} %copy-done) | data formatting | bytes 2097152
  45.1 0.0 copy-done.2
  45.1 0.6 %copy.21 = f32[8,128]{1,0:T(8,128)} copy(f32[8,128]{1,0:T(8,128)S(1)} %copy-done.2) | data formatting | bytes 8192
Async XLA Ops:
  40.2 2.4 %copy-start.1 = (f32[8,16,16,128]{3,2,1,0:T(8,128)S(1)}, f32[8,16,16,128]{3,2,1,0:T(8,128)}, u32[]{:S(2)}) copy-start(f32[8,16,16,128]{3,2,1,0:T(8,128)} %get-tuple-element.9) | copy-start | bytes 3145732
  42.5 1.6 %copy-start = (f32[8,16,16,128]{3,2,1,0:T(8,128)S(1)}, f32[8,16,16,128]{3,2,1,0:T(8,128)}, u32[]{:S(2)}) copy-start(f32[8,16,16,128]{3,2,1,0:T(8,128)} %get-tuple-element.10) | copy-start | bytes 3145732
  44.1 1.0 %copy-start.2 = (f32[8,128]{1,0:T(8,128)S(1)}, f32[8,128]{1,0:T(8,128)}, u32[]{:S(2)}) copy-start(f32[8,128]{1,0:T(8,128)} %get-tuple-element.11) | copy-start | bytes 12292

commit v2 on v1

--- a/solution.py
+++ b/solution.py
@@ -11,16 +11,17 @@
 TIME_STEP = 0.02
 MESH = pl.DeviceIdType.MESH
 LP, PR, SAT, Q1, Q2, P3 = range(6)
+HALVES = 2
 
 
 def kernel(
     ncell,
-    lp_hbm, pr_hbm, sat_hbm, sto_hbm, src_hbm, act_hbm, wells, obs, var, noise,
-    upd_out, pr_out, sat_out, pred_out,
-    lp, lp_peer, pr, sat, sto, src, act,
-    s, qa, qb, rhs, rbal, p3, snew, upd,
-    halo, act_halo, s_halo, q0_halo, found, wcol,
-    load_sems, out_sems, send_sems, recv_sems, act_send, act_recv,
+    lp_hbm, pr_hbm, sat_hbm, sto_hbm, src_hbm, act_hbm, wells,
+    lp, lp_peer, p3, snew, own_out, far_out,
+    pr, sat, sto, src, act,
+    s, qa, qb, rhs, rbal,
+    halo, act_halo, s_halo, q0_halo, found,
+    load_sems, send_sems, recv_sems, act_send, act_recv,
     peer_send, peer_recv, found_send, found_recv,
 ):
     md, nx, cy, cz = lp.shape
@@ -62,42 +63,48 @@
             device_id={"cell": to}, device_id_type=MESH,
         )
 
-    def edge_copy(f, side, ref):
+    half = md // HALVES
+    groups = [pl.ds(g * half, half) for g in range(HALVES)]
+
+    def edge_copy(f, side, ref, g):
         x = nx - 1 if side == 0 else 0
         to = right if side == 0 else left
-        return remote(ref.at[:, x], halo.at[f, side], send_sems.at[f, side], recv_sems.at[f, side], to)
+        part = groups[g]
+        return remote(
+            ref.at[part, x], halo.at[f, side, part], send_sems.at[f, side, g], recv_sems.at[f, side, g], to
+        )
 
     def act_copy(side):
         x = nx - 1 if side == 0 else 0
         to = right if side == 0 else left
         return remote(act_hbm.at[x], act_halo.at[side], act_send.at[side], act_recv.at[side], to)
 
-    def send_edges(f, ref):
+    def send_edges(f, ref, g):
         @pl.when(has_left)
         def _():
-            edge_copy(f, 1, ref).start()
+            edge_copy(f, 1, ref, g).start()
 
         @pl.when(has_right)
         def _():
-            edge_copy(f, 0, ref).start()
-
-    def wait_edges(f, ref):
+            edge_copy(f, 0, ref, g).start()
+
+    def wait_edges(f, ref, g):
         @pl.when(has_left)
         def _():
-            edge_copy(f, 0, ref).wait_recv()
+            edge_copy(f, 0, ref, g).wait_recv()
 
         @pl.when(has_right)
         def _():
-            edge_copy(f, 1, ref).wait_recv()
-
-    def sent_edges(f, ref):
+            edge_copy(f, 1, ref, g).wait_recv()
+
+    def sent_edges(f, ref, g):
         @pl.when(has_left)
         def _():
-            edge_copy(f, 1, ref).wait_send()
+            edge_copy(f, 1, ref, g).wait_send()
 
         @pl.when(has_right)
         def _():
-            edge_copy(f, 0, ref).wait_send()
+            edge_copy(f, 0, ref, g).wait_send()
 
     @pl.when(has_left)
     def _():
@@ -107,9 +114,11 @@
     def _():
         act_copy(0).start()
 
-    send_edges(LP, lp_hbm)
-    send_edges(PR, pr_hbm)
-    send_edges(SAT, sat_hbm)
+    for g in range(HALVES):
+        send_edges(LP, lp_hbm, g)
+        send_edges(PR, pr_hbm, g)
+    for g in range(HALVES):
+        send_edges(SAT, sat_hbm, g)
     peer = pltpu.make_async_remote_copy(
         src_ref=lp_hbm, dst_ref=lp_peer, send_sem=peer_send, recv_sem=peer_recv,
         device_id={"member": other}, device_id_type=MESH,
@@ -166,69 +175,73 @@
 
     lax.fori_loop(0, nx, prepare, 0)
 
-    def balance_at(x, below, above):
-        sc = s[:, x]
+    def balance_at(m, x, below, above):
+        sc = s[m, x]
         total = sto[x][None] + sc * (below + above + plane_sum(sc))
-        rbal[:, x] = 1.0 / total
-
-    def sweep_at(x, below, above, old, new, last):
-        sc = s[:, x]
-        p = (rhs[:, x] + sc * (below + above + plane_sum(old[:, x]))) * rbal[:, x]
-        new[:, x] = p if last else sc * p
+        rbal[m, x] = 1.0 / total
+
+    def sweep_at(m, x, below, above, old, new, last):
+        sc = s[m, x]
+        p = (rhs[m, x] + sc * (below + above + plane_sum(old[m, x]))) * rbal[m, x]
+        new[m, x] = p if last else sc * p
+
+    inner = nx - 2
+    width = max(d for d in range(1, 8) if inner % d == 0)
 
     def interior(f):
-        def step(x, carry):
-            f(x)
+        def step(i, carry):
+            for j in range(width):
+                f(1 + i * width + j)
             return carry
 
-        lax.fori_loop(1, nx - 1, step, 0)
-
-    def first_inside(x):
-        balance_at(x, s[:, x - 1], s[:, x + 1])
-        sweep_at(x, qa[:, x - 1], qa[:, x + 1], qa, qb, False)
-
-    interior(first_inside)
-
-    for side, there in ((0, has_left), (1, has_right)):
-        @pl.when(there)
-        def _(side=side):
-            act_copy(side).wait_recv()
-            edge_copy(LP, side, lp_hbm).wait_recv()
-            edge_copy(PR, side, pr_hbm).wait_recv()
-            s_halo[side] = act_halo[side].astype(jnp.float32)[None] * jnp.exp(0.5 * halo[LP, side])
-
-        q0_halo[side] = s_halo[side] * halo[PR, side]
+        lax.fori_loop(0, inner // width, step, 0)
 
     end = nx - 1
-    balance_at(0, s_halo[0], s[:, 1])
-    sweep_at(0, q0_halo[0], qa[:, 1], qa, qb, False)
-    balance_at(end, s[:, end - 1], s_halo[1])
-    sweep_at(end, qa[:, end - 1], q0_halo[1], qa, qb, False)
-    send_edges(Q1, qb)
-
-    interior(lambda x: sweep_at(x, qb[:, x - 1], qb[:, x + 1], qb, qa, False))
-    wait_edges(Q1, qb)
-    sweep_at(0, halo[Q1, 0], qb[:, 1], qb, qa, False)
-    sweep_at(end, qb[:, end - 1], halo[Q1, 1], qb, qa, False)
-    send_edges(Q2, qa)
-
-    interior(lambda x: sweep_at(x, qa[:, x - 1], qa[:, x + 1], qa, p3, True))
-    wait_edges(Q2, qa)
-    sweep_at(0, halo[Q2, 0], qa[:, 1], qa, p3, True)
-    sweep_at(end, qa[:, end - 1], halo[Q2, 1], qa, p3, True)
-    send_edges(P3, p3)
-    put_p = pltpu.make_async_copy(p3, pr_out, out_sems.at[0])
-    put_p.start()
+
+    def first_inside(m):
+        def f(x):
+            balance_at(m, x, s[m, x - 1], s[m, x + 1])
+            sweep_at(m, x, qa[m, x - 1], qa[m, x + 1], qa, qb, False)
+
+        interior(f)
+
+    for m in groups:
+        first_inside(m)
+
+    for g, m in enumerate(groups):
+        for side, there in ((0, has_left), (1, has_right)):
+            @pl.when(there)
+            def _(side=side, g=g, m=m):
+                if g == 0:
+                    act_copy(side).wait_recv()
+                edge_copy(LP, side, lp_hbm, g).wait_recv()
+                edge_copy(PR, side, pr_hbm, g).wait_recv()
+                s_halo[side, m] = act_halo[side].astype(jnp.float32)[None] * jnp.exp(0.5 * halo[LP, side, m])
+
+            q0_halo[side, m] = s_halo[side, m] * halo[PR, side, m]
+        balance_at(m, 0, s_halo[0, m], s[m, 1])
+        sweep_at(m, 0, q0_halo[0, m], qa[m, 1], qa, qb, False)
+        balance_at(m, end, s[m, end - 1], s_halo[1, m])
+        sweep_at(m, end, qa[m, end - 1], q0_halo[1, m], qa, qb, False)
+        send_edges(Q1, qb, g)
+
+    for f, old, new, nf, last in ((Q1, qb, qa, Q2, False), (Q2, qa, p3, P3, True)):
+        for g, m in enumerate(groups):
+            interior(lambda x: sweep_at(m, x, old[m, x - 1], old[m, x + 1], old, new, last))
+            wait_edges(f, old, g)
+            sweep_at(m, 0, halo[f, 0, m], old[m, 1], old, new, last)
+            sweep_at(m, end, old[m, end - 1], halo[f, 1, m], old, new, last)
+            send_edges(nf, new, g)
     loads[5].wait()
 
     def face(sn, pn, tn, pc, tc):
         d = pn - pc
         return sn * (d * jnp.where(d > 0, tn, tc))
 
-    def saturate_at(x, below, above):
-        sc = s[:, x]
-        pc = p3[:, x]
-        raw = sat[:, x]
+    def saturate_at(m, x, below, above):
+        sc = s[m, x]
+        pc = p3[m, x]
+        raw = sat[m, x]
         tc = raw * raw
         bs, bp, bt = below
         as_, ap, at = above
@@ -236,12 +249,13 @@
         gz = sc * face(jnp.where(lane == cz - 1, 0.0, z_up(sc)), z_up(pc), z_up(tc), pc, tc)
         gy = sc * face(jnp.where(row == cy - 1, 0.0, y_up(sc)), y_up(pc), y_up(tc), pc, tc)
         change = sc * change + (gz - z_down(gz)) + (gy - y_down(gy))
-        snew[:, x] = raw + change * (TIME_STEP / sto[x])[None]
-
-    def at_x(x):
-        return s[:, x], p3[:, x], sat[:, x]
-
-    interior(lambda x: saturate_at(x, at_x(x - 1), at_x(x + 1)))
+        snew[m, x] = raw + change * (TIME_STEP / sto[x])[None]
+
+    def at_x(m, x):
+        return s[m, x], p3[m, x], sat[m, x]
+
+    for m in groups:
+        interior(lambda x: saturate_at(m, x, at_x(m, x - 1), at_x(m, x + 1)))
 
     nw = wells.shape[0]
     cells_dev = nx * cy * cz
@@ -265,12 +279,11 @@
 
     acc = lax.fori_loop(0, nw, gather(p3_rows, 0), jnp.zeros((md, 2 * nw), jnp.float32), unroll=8)
 
-    wait_edges(SAT, sat_hbm)
-    wait_edges(P3, p3)
-    saturate_at(0, (s_halo[0], halo[P3, 0], halo[SAT, 0]), at_x(1))
-    saturate_at(end, at_x(end - 1), (s_halo[1], halo[P3, 1], halo[SAT, 1]))
-    put_s = pltpu.make_async_copy(snew, sat_out, out_sems.at[1])
-    put_s.start()
+    for g, m in enumerate(groups):
+        wait_edges(SAT, sat_hbm, g)
+        wait_edges(P3, p3, g)
+        saturate_at(m, 0, (s_halo[0, m], halo[P3, 0, m], halo[SAT, 0, m]), at_x(m, 1))
+        saturate_at(m, end, at_x(m, end - 1), (s_halo[1, m], halo[P3, 1, m], halo[SAT, 1, m]))
     acc = lax.fori_loop(0, nw, gather(sn_rows, nw), acc, unroll=8)
     found[0, 0] = acc
 
@@ -302,10 +315,41 @@
     for k in range(1, ncell):
         own = own + found[0, k]
         far = far + found[1, k]
+    own_out[...] = own
+    far_out[...] = far
+
+    peer.wait_recv()
+    peer.wait_send()
+    each_found(lambda c: c.wait_send())
+    for f, ref in ((LP, lp_hbm), (PR, pr_hbm), (SAT, sat_hbm), (Q1, qb), (Q2, qa), (P3, p3)):
+        for g in range(HALVES):
+            sent_edges(f, ref, g)
+
+    @pl.when(has_left)
+    def _():
+        act_copy(1).wait_send()
+
+    @pl.when(has_right)
+    def _():
+        act_copy(0).wait_send()
+
+
+def update_kernel(
+    lp, lp_peer, p3, snew, own_in, far_in, obs, var, noise,
+    upd_out, pr_out, sat_out, pred_out,
+    upd, wcol, out_sems,
+):
+    md, nx, cy, cz = lp.shape
+    put_p = pltpu.make_async_copy(p3, pr_out, out_sems.at[0])
+    put_s = pltpu.make_async_copy(snew, sat_out, out_sems.at[1])
+    put_p.start()
+    put_s.start()
+    mem = lax.axis_index("member")
+    own = own_in[...]
+    far = far_in[...]
     pred_out[...] = own
-
+    nd = own.shape[1]
     members = 2 * md
-    nd = 2 * nw
     root = float(members - 1) ** 0.5
     both = jnp.concatenate([own, far], axis=0)
     spread = (both - jnp.mean(both, axis=0, keepdims=True)) * (1.0 / root)
@@ -326,7 +370,6 @@
     for j in range(md):
         wcol[j] = jnp.broadcast_to(aug[:, members + j : members + j + 1] * (1.0 / root), (members, cz))
 
-    peer.wait_recv()
     parts = 4
     share = nx // parts
 
@@ -347,20 +390,6 @@
     for i in range(parts):
         lax.fori_loop(i * share, (i + 1) * share, mix, 0)
         put_u(i).start()
-
-    each_found(lambda c: c.wait_send())
-    peer.wait_send()
-    for f, ref in ((LP, lp_hbm), (PR, pr_hbm), (SAT, sat_hbm), (Q1, qb), (Q2, qa), (P3, p3)):
-        sent_edges(f, ref)
-
-    @pl.when(has_left)
-    def _():
-        act_copy(1).wait_send()
-
-    @pl.when(has_right)
-    def _():
-        act_copy(0).wait_send()
-
     put_p.wait()
     put_s.wait()
     for i in range(parts):
@@ -376,32 +405,38 @@
     field = (md, nx, cy, cz)
     plane = (nx, cy, cz)
     f32 = jnp.float32
-    any_spec = pl.BlockSpec(memory_space=pl.ANY)
+    any_spec = pl.BlockSpec(memory_space=pltpu.HBM)
     vmem_spec = pl.BlockSpec(memory_space=pltpu.VMEM)
     dma = pltpu.SemaphoreType.DMA
-    return pl.pallas_call(
+    limit = 24 * 1024 * 1024
+    lp, lp_peer, p3, snew, own, far = pl.pallas_call(
         functools.partial(kernel, ncell),
-        out_shape=[jax.ShapeDtypeStruct(field, f32)] * 3 + [jax.ShapeDtypeStruct((md, nd), f32)],
-        in_specs=[any_spec] * 6 + [pl.BlockSpec(memory_space=pltpu.SMEM)] + [vmem_spec] * 3,
-        out_specs=[any_spec] * 3 + [vmem_spec],
+        out_shape=[pltpu.VMEM(field, f32)] * 4 + [pltpu.VMEM((md, nd), f32)] * 2,
+        in_specs=[any_spec] * 6 + [pl.BlockSpec(memory_space=pltpu.SMEM)],
+        out_specs=[vmem_spec] * 6,
         scratch_shapes=[
-            pltpu.VMEM(field, f32), pltpu.VMEM(field, f32), pltpu.VMEM(field, f32), pltpu.VMEM(field, f32),
+            pltpu.VMEM(field, f32), pltpu.VMEM(field, f32),
             pltpu.VMEM(plane, f32), pltpu.VMEM(plane, f32), pltpu.VMEM(plane, jnp.int32),
-            *[pltpu.VMEM(field, f32) for _ in range(8)],
+            *[pltpu.VMEM(field, f32) for _ in range(5)],
             pltpu.VMEM((6, 2, md, cy, cz), f32),
             pltpu.VMEM((2, cy, cz), jnp.int32),
             pltpu.VMEM((2, md, cy, cz), f32),
             pltpu.VMEM((2, md, cy, cz), f32),
             pltpu.VMEM((2, ncell, md, nd), f32),
-            pltpu.VMEM((md, 2 * md, cz), f32),
-            dma((6,)), dma((6,)), dma((6, 2)), dma((6, 2)), dma((2,)), dma((2,)),
+            dma((6,)), dma((6, 2, HALVES)), dma((6, 2, HALVES)), dma((2,)), dma((2,)),
             dma, dma, dma((2, ncell)), dma((2, ncell)),
         ],
-        compiler_params=pltpu.CompilerParams(
-            collective_id=0, has_side_effects=True, vmem_limit_bytes=58 * 1024 * 1024
-        ),
+        compiler_params=pltpu.CompilerParams(collective_id=0, has_side_effects=True, vmem_limit_bytes=limit),
+    )(log_perm, pressure, saturation, storage, source, active, wells)
+    return pl.pallas_call(
+        update_kernel,
+        out_shape=[jax.ShapeDtypeStruct(field, f32)] * 3 + [jax.ShapeDtypeStruct((md, nd), f32)],
+        in_specs=[vmem_spec] * 9,
+        out_specs=[pl.BlockSpec(memory_space=pltpu.HBM)] * 3 + [vmem_spec],
+        scratch_shapes=[pltpu.VMEM(field, f32), pltpu.VMEM((md, 2 * md, cz), f32), dma((6,))],
+        compiler_params=pltpu.CompilerParams(vmem_limit_bytes=limit),
     )(
-        log_perm, pressure, saturation, storage, source, active, wells,
+        lp, lp_peer, p3, snew, own, far,
         observed.reshape(1, nd), observation_variance.reshape(1, nd), noise,
     )
 

time: 45.9 us -> 47.9 us (1.044)
  local copies, waits for them, and re-layouts: 5.53 us -> 7.71 us
    unnamed x10 -> x20, local copies, waits for them, and re-layouts: 5.53 us -> 7.71 us
    pallas_call x1 -> x2, Pallas kernels: 39.5 us -> 39.2 us  [the longest x1 34.9 us: local(): pl.pallas_call(functools.partial(kernel, ncell), out_shape=[pltpu.VMEM(fi...]
where the time goes in v2:
time: 47.9 us; the launch traced here: 47.6 us
  Pallas kernels  39.2 us (82%)
  local copies, waits for them, and re-layouts  7.71 us (16%)
  between operations  0.68 us (1%)
    pallas_call x1, Pallas kernels, local(): pl.pallas_call(functools.partial(kernel, ncell), out_shape=[pltpu.VMEM(fi...  34.9 us
    unnamed x20, local copies, waits for them, and re-layouts  7.71 us
    pallas_call x1, Pallas kernels, local(): pl.pallas_call(update_kernel, out_shape=[jax.ShapeDtypeStruct(field, f32)...  4.25 us

profile of v2, /device:TPU:0, one launch (start us, length us, event | category | flops | bytes accessed | tf_op | source)
XLA Modules:
  0.0 47.6 jit_solution(13351075351601491164)
XLA Ops:
  0.6 0.0 copy-start.9
  0.6 0.6 %copy-done.9 = s32[64]{0:T(128)S(1)} copy-done((s32[64]{0:T(128)S(1)}, s32[64]{0:T(128)}, u32[]{:S(2)}) %copy-start.9) | copy-done | bytes 280
  1.3 0.0 copy-start
  1.3 1.2 %copy-done = f32[8,16,16,128]{3,2,1,0:T(8,128)S(1)} copy-done((f32[8,16,16,128]{3,2,1,0:T(8,128)S(1)}, f32[8,16,16,128]{3,2,1,0:T(8,128)}, u32[]{:S(2)}) %copy-start) | copy-done | bytes 1048600
  2.5 0.0 copy-start.1
  2.5 1.2 %copy-done.1 = f32[8,16,16,128]{3,2,1,0:T(8,128)S(1)} copy-done((f32[8,16,16,128]{3,2,1,0:T(8,128)S(1)}, f32[8,16,16,128]{3,2,1,0:T(8,128)}, u32[]{:S(2)}) %copy-start.1) | copy-done | bytes 1048600
  3.7 0.0 copy-start.2
  3.7 1.2 %copy-done.2 = f32[8,16,16,128]{3,2,1,0:T(8,128)S(1)} copy-done((f32[8,16,16,128]{3,2,1,0:T(8,128)S(1)}, f32[8,16,16,128]{3,2,1,0:T(8,128)}, u32[]{:S(2)}) %copy-start.2) | copy-done | bytes 1048600
  5.0 0.0 copy-start.3
  5.0 0.9 %copy-done.3 = f32[16,16,128]{2,1,0:T(8,128)S(1)} copy-done((f32[16,16,128]{2,1,0:T(8,128)S(1)}, f32[16,16,128]{2,1,0:T(8,128)}, u32[]{:S(2)}) %copy-start.3) | copy-done | bytes 131096
  5.9 0.0 copy-start.4
  5.9 0.9 %copy-done.4 = f32[16,16,128]{2,1,0:T(8,128)S(1)} copy-done((f32[16,16,128]{2,1,0:T(8,128)S(1)}, f32[16,16,128]{2,1,0:T(8,128)}, u32[]{:S(2)}) %copy-start.4) | copy-done | bytes 131096
  6.8 0.0 copy-start.5
  6.8 0.9 %copy-done.5 = s32[16,16,128]{2,1,0:T(8,128)S(1)} copy-done((s32[16,16,128]{2,1,0:T(8,128)S(1)}, s32[16,16,128]{2,1,0:T(8,128)}, u32[]{:S(2)}) %copy-start.5) | copy-done | bytes 131096
  7.7 34.9 %shard_map.129 = (f32[8,16,16,128]{3,2,1,0:T(8,128)S(1)}, f32[8,16,16,128]{3,2,1,0:T(8,128)S(1)}, f32[8,16,16,128]{3,2,1,0:T(8,128)S(1)}, f32[8,16,16,128]{3,2,1...) custom-call(f32[8,16,16,128]{3,2,1,0:T(8,128)S(1)} %copy-done, f32[8,16,16,128]{3,2,1,0:T(8,128)S(1)} %copy-done.1, ...), custom_call_target="tpu_custom_call" | custom-call | tf_op jit(solution)/shard_map/pallas_call | solution.py:412
  42.6 0.0 copy-start.6
  42.6 0.0 copy-start.7
  42.6 0.0 copy-start.8
  42.6 0.7 %copy-done.6 = f32[16,128]{1,0:T(8,128)S(1)} copy-done((f32[16,128]{1,0:T(8,128)S(1)}, f32[16,128]{1,0:T(8,128)}, u32[]{:S(2)}) %copy-start.6) | copy-done | bytes 8216
  43.3 0.0 copy-done.7
  43.3 0.0 copy-done.8
  43.3 4.2 %shard_map.130 = (f32[8,16,16,128]{3,2,1,0:T(8,128)}, f32[8,16,16,128]{3,2,1,0:T(8,128)}, f32[8,16,16,128]{3,2,1,0:T(8,128)}, f32[8,128]{1,0:T(8,128)}) custom-call(f32[8,16,16,128]{3,2,1,0:T(8,128)S(1)} %get-tuple-element.10.lp, f32[8,16,16,128]{3,2,1,0:T(8,128)S(1)} %get-tuple-element.11.lp_peer, f32[8,16,16,128]{3,2,1,0:T(8,128)S(1)} %get-tuple-element.12.p3, ...), custom_call_target="tpu_custom_call" | custom-call | tf_op jit(solution)/shard_map/pallas_call | solution.py:431
Async XLA Ops:
  0.6 0.7 %copy-start.9 = (s32[64]{0:T(128)S(1)}, s32[64]{0:T(128)}, u32[]{:S(2)}) copy-start(s32[64]{0:T(128)} %wells.1) | copy-start | bytes 772
  1.3 1.2 %copy-start = (f32[8,16,16,128]{3,2,1,0:T(8,128)S(1)}, f32[8,16,16,128]{3,2,1,0:T(8,128)}, u32[]{:S(2)}) copy-start(f32[8,16,16,128]{3,2,1,0:T(8,128)} %lp_hbm.1) | copy-start | bytes 3145732
  2.5 1.2 %copy-start.1 = (f32[8,16,16,128]{3,2,1,0:T(8,128)S(1)}, f32[8,16,16,128]{3,2,1,0:T(8,128)}, u32[]{:S(2)}) copy-start(f32[8,16,16,128]{3,2,1,0:T(8,128)} %pr_hbm.1) | copy-start | bytes 3145732
  3.7 1.2 %copy-start.2 = (f32[8,16,16,128]{3,2,1,0:T(8,128)S(1)}, f32[8,16,16,128]{3,2,1,0:T(8,128)}, u32[]{:S(2)}) copy-start(f32[8,16,16,128]{3,2,1,0:T(8,128)} %sat_hbm.1) | copy-start | bytes 3145732
  5.0 0.9 %copy-start.3 = (f32[16,16,128]{2,1,0:T(8,128)S(1)}, f32[16,16,128]{2,1,0:T(8,128)}, u32[]{:S(2)}) copy-start(f32[16,16,128]{2,1,0:T(8,128)} %sto_hbm.1) | copy-start | bytes 393220
  5.9 0.9 %copy-start.4 = (f32[16,16,128]{2,1,0:T(8,128)S(1)}, f32[16,16,128]{2,1,0:T(8,128)}, u32[]{:S(2)}) copy-start(f32[16,16,128]{2,1,0:T(8,128)} %src_hbm.1) | copy-start | bytes 393220
  6.8 0.9 %copy-start.5 = (s32[16,16,128]{2,1,0:T(8,128)S(1)}, s32[16,16,128]{2,1,0:T(8,128)}, u32[]{:S(2)}) copy-start(s32[16,16,128]{2,1,0:T(8,128)} %act_hbm.1) | copy-start | bytes 393220
  42.6 0.7 %copy-start.6 = (f32[16,128]{1,0:T(8,128)S(1)}, f32[16,128]{1,0:T(8,128)}, u32[]{:S(2)}) copy-start(f32[16,128]{1,0:T(8,128)} %noise.1) | copy-start | bytes 24580
  42.6 0.7 %copy-start.7 = (f32[128]{0:T(128)S(1)}, f32[128]{0:T(128)}, u32[]{:S(2)}) copy-start(f32[128]{0:T(128)} %param.17) | copy-start | bytes 1540
  42.6 0.7 %copy-start.8 = (f32[128]{0:T(128)S(1)}, f32[128]{0:T(128)}, u32[]{:S(2)}) copy-start(f32[128]{0:T(128)} %param.18) | copy-start | bytes 1540

commit v3 on v2

--- a/solution.py
+++ b/solution.py
@@ -337,9 +337,15 @@
 def update_kernel(
     lp, lp_peer, p3, snew, own_in, far_in, obs, var, noise,
     upd_out, pr_out, sat_out, pred_out,
-    upd, wcol, out_sems,
+    upd, wcol, obs_v, var_v, noise_v, out_sems, in_sems,
 ):
     md, nx, cy, cz = lp.shape
+    gets = [
+        pltpu.make_async_copy(a, b, in_sems.at[i])
+        for i, (a, b) in enumerate([(obs, obs_v), (var, var_v), (noise, noise_v)])
+    ]
+    for c in gets:
+        c.start()
     put_p = pltpu.make_async_copy(p3, pr_out, out_sems.at[0])
     put_s = pltpu.make_async_copy(snew, sat_out, out_sems.at[1])
     put_p.start()
@@ -353,9 +359,11 @@
     root = float(members - 1) ** 0.5
     both = jnp.concatenate([own, far], axis=0)
     spread = (both - jnp.mean(both, axis=0, keepdims=True)) * (1.0 / root)
-    dvar = INFLATION_FACTOR * var[...]
+    for c in gets:
+        c.wait()
+    dvar = INFLATION_FACTOR * var_v[...]
     first = pl.multiple_of(mem * md, md)
-    misfit = obs[...] + jnp.sqrt(dvar) * noise[pl.ds(first, md), :] - own
+    misfit = obs_v[...] + jnp.sqrt(dvar) * noise_v[pl.ds(first, md), :] - own
     stack = jnp.concatenate([spread, misfit, jnp.zeros((nd - 3 * md, nd), jnp.float32)], axis=0)
     aug = lax.dot_general(
         spread / dvar, stack, (((1,), (1,)), ((), ())),
@@ -408,7 +416,6 @@
     any_spec = pl.BlockSpec(memory_space=pltpu.HBM)
     vmem_spec = pl.BlockSpec(memory_space=pltpu.VMEM)
     dma = pltpu.SemaphoreType.DMA
-    limit = 24 * 1024 * 1024
     lp, lp_peer, p3, snew, own, far = pl.pallas_call(
         functools.partial(kernel, ncell),
         out_shape=[pltpu.VMEM(field, f32)] * 4 + [pltpu.VMEM((md, nd), f32)] * 2,
@@ -426,15 +433,18 @@
             dma((6,)), dma((6, 2, HALVES)), dma((6, 2, HALVES)), dma((2,)), dma((2,)),
             dma, dma, dma((2, ncell)), dma((2, ncell)),
         ],
-        compiler_params=pltpu.CompilerParams(collective_id=0, has_side_effects=True, vmem_limit_bytes=limit),
+        compiler_params=pltpu.CompilerParams(collective_id=0, has_side_effects=True, vmem_limit_bytes=58 * 1024 * 1024),
     )(log_perm, pressure, saturation, storage, source, active, wells)
     return pl.pallas_call(
         update_kernel,
         out_shape=[jax.ShapeDtypeStruct(field, f32)] * 3 + [jax.ShapeDtypeStruct((md, nd), f32)],
-        in_specs=[vmem_spec] * 9,
+        in_specs=[vmem_spec] * 6 + [any_spec] * 3,
         out_specs=[pl.BlockSpec(memory_space=pltpu.HBM)] * 3 + [vmem_spec],
-        scratch_shapes=[pltpu.VMEM(field, f32), pltpu.VMEM((md, 2 * md, cz), f32), dma((6,))],
-        compiler_params=pltpu.CompilerParams(vmem_limit_bytes=limit),
+        scratch_shapes=[
+            pltpu.VMEM(field, f32), pltpu.VMEM((md, 2 * md, cz), f32),
+            pltpu.VMEM((1, nd), f32), pltpu.VMEM((1, nd), f32), pltpu.VMEM((2 * md, nd), f32), dma((6,)), dma((3,)),
+        ],
+        compiler_params=pltpu.CompilerParams(vmem_limit_bytes=24 * 1024 * 1024),
     )(
         lp, lp_peer, p3, snew, own, far,
         observed.reshape(1, nd), observation_variance.reshape(1, nd), noise,

time: 47.9 us -> 40.3 us (0.84)
  local copies, waits for them, and re-layouts: 7.71 us -> 0.68 us
    unnamed x20 -> x6, local copies, waits for them, and re-layouts: 7.71 us -> 0.68 us
where the time goes in v3:
time: 40.3 us; the launch traced here: 40.1 us
  Pallas kernels  38.8 us (96%)
  local copies, waits for them, and re-layouts  0.68 us (2%)
  between operations  0.67 us (2%)
    pallas_call x1, Pallas kernels, local(): pl.pallas_call(functools.partial(kernel, ncell), out_shape=[pltpu.VMEM(fi...  34.5 us
    pallas_call x1, Pallas kernels, local(): pl.pallas_call(update_kernel, out_shape=[jax.ShapeDtypeStruct(field, f32)...  4.26 us

profile of v3, /device:TPU:0, one launch (start us, length us, event | category | flops | bytes accessed | tf_op | source)
XLA Modules:
  0.0 40.1 jit_solution(12513157441584786673)
XLA Ops:
  0.6 34.5 %shard_map.129 = (f32[8,16,16,128]{3,2,1,0:T(8,128)S(1)}, f32[8,16,16,128]{3,2,1,0:T(8,128)S(1)}, f32[8,16,16,128]{3,2,1,0:T(8,128)S(1)}, f32[8,16,16,128]{3,2,1...) custom-call(f32[8,16,16,128]{3,2,1,0:T(8,128)} %lp_hbm.1, f32[8,16,16,128]{3,2,1,0:T(8,128)} %pr_hbm.1, ...), custom_call_target="tpu_custom_call" | custom-call | tf_op jit(solution)/shard_map/pallas_call | solution.py:419
  35.2 0.0 copy-start
  35.2 0.0 copy-start.1
  35.2 0.0 copy-start.2
  35.2 0.7 %copy-done = f32[16,128]{1,0:T(8,128)S(1)} copy-done((f32[16,128]{1,0:T(8,128)S(1)}, f32[16,128]{1,0:T(8,128)}, u32[]{:S(2)}) %copy-start) | copy-done | bytes 8216
  35.9 0.0 copy-done.1
  35.9 0.0 copy-done.2
  35.9 4.3 %shard_map.130 = (f32[8,16,16,128]{3,2,1,0:T(8,128)}, f32[8,16,16,128]{3,2,1,0:T(8,128)}, f32[8,16,16,128]{3,2,1,0:T(8,128)}, f32[8,128]{1,0:T(8,128)}) custom-call(f32[8,16,16,128]{3,2,1,0:T(8,128)S(1)} %get-tuple-element.10.lp, f32[8,16,16,128]{3,2,1,0:T(8,128)S(1)} %get-tuple-element.11.lp_peer, f32[8,16,16,128]{3,2,1,0:T(8,128)S(1)} %get-tuple-element.12.p3, ...), custom_call_target="tpu_custom_call" | custom-call | tf_op jit(solution)/shard_map/pallas_call | solution.py:438
Async XLA Ops:
  35.2 0.7 %copy-start = (f32[16,128]{1,0:T(8,128)S(1)}, f32[16,128]{1,0:T(8,128)}, u32[]{:S(2)}) copy-start(f32[16,128]{1,0:T(8,128)} %noise.1) | copy-start | bytes 24580
  35.2 0.7 %copy-start.1 = (f32[128]{0:T(128)S(1)}, f32[128]{0:T(128)}, u32[]{:S(2)}) copy-start(f32[128]{0:T(128)} %param.17) | copy-start | bytes 1540
  35.2 0.7 %copy-start.2 = (f32[128]{0:T(128)S(1)}, f32[128]{0:T(128)}, u32[]{:S(2)}) copy-start(f32[128]{0:T(128)} %param.18) | copy-start | bytes 1540
